TPU v7x, 32 devices: a whole 2x2x4 slice. The times are simulated.
32 devices in a mesh: gx: 2 (over x), gy: 4 (over z), gz: 4 (over y, core).
Axes of the slice: x: 2, y: 2, z: 4, core: 2. Of those that a mesh axis runs over, the one named last changes fastest.
Arguments:
- pressure: float32 [2, 32, 32, 512], P(None, 'gx', 'gy', 'gz'), may hold values from -6 to 6
- saturation: float32 [3, 2, 32, 32, 512], P(None, None, 'gx', 'gy', 'gz'), may hold values from 0.15 to 0.45
- permeability: float32 [32, 32, 512], P('gx', 'gy', 'gz'), may hold values from 0.5 to 2
- porosity: float32 [32, 32, 512], P('gx', 'gy', 'gz'), may hold values from 0.1 to 0.35
- upwind_flags: int32 [32, 32, 512], P('gx', 'gy', 'gz'), may hold values from 0 to 63
- diag_inverse: float32 [2, 3, 3, 32, 32, 512], P(None, None, None, 'gx', 'gy', 'gz'), may hold values from -0.12 to 0.8, as said below
- seismic_obs: float32 [32, 32, 512], P('gx', 'gy', 'gz'), may hold values from -6 to 6
- well_x: int32 [2, 4, 64], P('gx', 'gy'), may hold values from 0 to 15
- well_y: int32 [2, 4, 64], P('gx', 'gy'), may hold values from 0 to 7
- well_top: int32 [2, 4, 64], P('gx', 'gy'), may hold values from 0 to 255
- well_len: int32 [2, 4, 64], P('gx', 'gy'), may hold values from 128 to 256
- well_bhp: float32 [2, 2, 4, 64], P(None, 'gx', 'gy'), may hold values from -3 to 3
- well_obs: float32 [2, 2, 4, 64], P(None, 'gx', 'gy'), may hold values from -48 to 48
- fault_cell: int32 [32, 16, 128], P(('gx', 'gy', 'gz')), may hold values from 0 to 16383
- fault_count: int32 [32, 16], P(('gx', 'gy', 'gz')), may hold values from 0 to 128, as said below
- fault_trans: float32 [32, 16, 128], P(('gx', 'gy', 'gz')), may hold values from 0.5 to 2, as said below
- fault_up: int32 [32, 16, 128], P(('gx', 'gy', 'gz')), may hold values from 0 to 3, as said below
- region_map: int32 [8, 8, 128], P('gx', 'gy', 'gz'), may hold values from 0 to 1023
Outputs:
- adjoint: float32 [2, 3, 32, 32, 512], P(None, None, 'gx', 'gy', 'gz')
- region_grad: float32 [2, 1024], P(None, ('gx', 'gy', 'gz'))
Inputs may be any that keep to these rules, and one draw needn't show every extreme that they name: fault_count[dev][p] equals fault_count[i * 16 + p][a] of the connection's other end; a device has no connections with itself; in every draw one device of each group of 16 has exactly 128 connections with every other device of its group. `fault_cell`: slot s of dev toward peer p and slot s of that peer toward dev are the two ends of one connection. `fault_trans`: both ends of a connection hold the same transmissibility. `fault_up`: the two ends of a connection hold opposite bits. `diag_inverse`: entries [t][0][0] lie in 0.25 to 0.5, entries [t][u][u] for u = 1, 2 in 0.4 to 0.8, all others in -0.12 to 0.12.
All inputs are finite; a program needn't handle non-finite values.
Results may differ from a plain program's by a relative error of at most 0.0001.
Values sent between devices are 32-bit elements; how exact they have to be, the bound alone decides.
A program may use at most 128 MiB of HBM per device.

v0:
```python
import jax
import jax.numpy as jnp
from jax import lax
from jax.sharding import PartitionSpec as P

ITERS = 6
BOX = 4
PARAM_REGIONS = 32
fluid_viscosity = (0.4, 0.5, 1.0)
sigma_sq = 64.0


def extended_2(block, sides, width):
    for axis, dim in sides:
        count = lax.axis_size(axis)
        forward = [(i, i + 1) for i in range(count - 1)]
        backward = [(target, source) for source, target in forward]
        low = lax.ppermute(
            lax.slice_in_dim(block, block.shape[dim] - width, None, axis=dim), axis, forward
        )
        high = lax.ppermute(lax.slice_in_dim(block, 0, width, axis=dim), axis, backward)
        block = jnp.concatenate([low, block, high], axis=dim)
    return block


def phase_mobility(water_sat, oil_sat):
    gas_sat = 1.0 - water_sat - oil_sat
    return jnp.stack(
        [
            water_sat * water_sat / fluid_viscosity[0],
            oil_sat * oil_sat / fluid_viscosity[1],
            gas_sat * gas_sat / fluid_viscosity[2],
        ]
    )


def mobility_slopes(water_sat, oil_sat):
    gas_sat = 1.0 - water_sat - oil_sat
    return (
        2.0 * water_sat / fluid_viscosity[0] - 2.0 * gas_sat / fluid_viscosity[2],
        2.0 * oil_sat / fluid_viscosity[1] - 2.0 * gas_sat / fluid_viscosity[2],
    )


def interior_strip(padded, direction):
    slicer = [slice(None), slice(1, -1), slice(1, -1), slice(1, -1)]
    slicer[direction + 1] = slice(None)
    return padded[tuple(slicer)]


def apply_inverse(inverse, residual):
    return jnp.sum(inverse * residual[:, None], axis=0)


def box_sums(quantity):
    shaped = quantity.reshape(
        quantity.shape[0] // BOX, BOX, quantity.shape[1] // BOX, BOX, quantity.shape[2] // BOX, BOX
    )
    return jnp.sum(shaped, axis=(1, 3, 5)).reshape(-1)


def fault_exchange(values):
    return lax.all_to_all(values, ("gy", "gz"), split_axis=1, concat_axis=1, tiled=True)


def fault_sum(lagrange, coefficient, cell_index):
    flattened = lagrange.reshape(lagrange.shape[0], -1)
    own_values = flattened[:, cell_index]
    arrived = fault_exchange(own_values)
    contribution = jnp.sum(coefficient * arrived, axis=0)
    faults = (
        jnp.zeros((flattened.shape[1],), jnp.float32)
        .at[cell_index.reshape(-1)]
        .add(contribution.reshape(-1))
    )
    return faults.reshape(lagrange.shape[1:])


def neighbour_terms(lagrange, ahead_list, behind_list, want_local):
    padded = extended_2(lagrange, (("gx", 1), ("gy", 2), ("gz", 3)), 1)
    upper_terms = []
    lower_terms = []
    for direction in range(3):
        stripe = interior_strip(padded, direction)
        length = lagrange.shape[direction + 1]
        upper_terms.append(
            jnp.sum(
                ahead_list[direction] * lax.slice_in_dim(stripe, 2, length + 2, axis=direction + 1),
                axis=0,
            )
        )
        lower_terms.append(
            jnp.sum(
                behind_list[direction] * lax.slice_in_dim(stripe, 0, length, axis=direction + 1),
                axis=0,
            )
        )
    local_ahead = None
    local_behind = None
    if want_local:
        local_ahead = [jnp.sum(coefficient * lagrange, axis=0) for coefficient in ahead_list]
        local_behind = [jnp.sum(coefficient * lagrange, axis=0) for coefficient in behind_list]
    return (upper_terms, lower_terms, local_ahead, local_behind)


def local(
    pressure,
    saturation,
    permeability,
    porosity,
    upwind_flags,
    diag_inverse,
    seismic_obs,
    well_x,
    well_y,
    well_top,
    well_len,
    well_bhp,
    well_obs,
    fault_cell,
    fault_count,
    fault_trans,
    fault_up,
    region_map,
):
    mobility = [
        phase_mobility(saturation[step_index + 1, 0], saturation[step_index + 1, 1])
        for step_index in range(2)
    ]
    flag_field = upwind_flags.astype(jnp.float32)[None]
    bundle = jnp.concatenate(
        [permeability[None], mobility[0], mobility[1], flag_field, pressure], axis=0
    )
    padded = extended_2(bundle, (("gx", 1), ("gy", 2), ("gz", 3)), 1)
    ahead_coef = [[], []]
    behind_coef = [[], []]
    pressure_ahead = [[], []]
    pressure_trailing = [[], []]
    for direction in range(3):
        stripe = interior_strip(padded, direction)
        length = permeability.shape[direction]
        lower_side = lax.slice_in_dim(stripe, 0, length + 1, axis=direction + 1)
        upper_side = lax.slice_in_dim(stripe, 1, length + 2, axis=direction + 1)
        face_trans = jnp.sqrt(lower_side[0] * upper_side[0])
        lower_flags = lower_side[7].astype(jnp.int32)
        for step_index in range(2):
            first = 1 + 3 * step_index
            upwind_bit = jnp.bitwise_and(
                jnp.right_shift(lower_flags, 3 * step_index + direction), 1
            )
            chosen = jnp.where(
                upwind_bit[None] == 1, lower_side[first : first + 3], upper_side[first : first + 3]
            )
            extended = face_trans[None] * chosen
            ahead_coef[step_index].append(
                lax.slice_in_dim(extended, 1, length + 1, axis=direction + 1)
            )
            behind_coef[step_index].append(
                lax.slice_in_dim(extended, 0, length, axis=direction + 1)
            )
            pressure_stripe = stripe[8 + step_index]
            pressure_ahead[step_index].append(
                lax.slice_in_dim(pressure_stripe, 2, length + 2, axis=direction)
            )
            pressure_trailing[step_index].append(
                lax.slice_in_dim(pressure_stripe, 0, length, axis=direction)
            )
    cell_index = fault_cell[0]
    live_slots = (
        jnp.arange(cell_index.shape[1], dtype=jnp.int32)[None, :] < fault_count[0][:, None]
    ).astype(jnp.float32)
    own_mobility = jnp.concatenate(mobility, axis=0).reshape(6, -1)[:, cell_index]
    peer_mobility = lax.all_to_all(
        own_mobility, ("gy", "gz"), split_axis=1, concat_axis=1, tiled=True
    )
    fault_coef = []
    for step_index in range(2):
        upwind_bit = jnp.bitwise_and(jnp.right_shift(fault_up[0], step_index), 1)
        first = 3 * step_index
        chosen = jnp.where(
            upwind_bit[None] == 1, own_mobility[first : first + 3], peer_mobility[first : first + 3]
        )
        fault_coef.append(fault_trans[0][None] * chosen * live_slots[None])
    column_x = well_x[0, 0]
    column_y = well_y[0, 0]
    depth_count = permeability.shape[2]
    depth_index = (lax.axis_index("gz") * depth_count + jnp.arange(depth_count, dtype=jnp.int32))[
        None, :
    ]
    top_cells = well_top[0, 0][:, None]
    perforated = (
        (depth_index >= top_cells) & (depth_index < top_cells + well_len[0, 0][:, None])
    ).astype(jnp.float32)
    column_perm = permeability[column_x, column_y]
    partial_rates = []
    column_data = []
    for step_index in range(2):
        column_pressure = pressure[step_index][column_x, column_y]
        column_total = jnp.sum(mobility[step_index][:, column_x, column_y], axis=0)
        drawdown = column_pressure - well_bhp[step_index, 0, 0][:, None]
        partial_rates.append(jnp.sum(perforated * column_perm * column_total * drawdown, axis=1))
        column_data.append((column_total, drawdown))
    well_flow_rates = lax.psum(jnp.stack(partial_rates), "gz")
    misfit = (well_flow_rates - well_obs[:, 0, 0]) / sigma_sq
    sources = []
    explicit = jnp.zeros(permeability.shape, jnp.float32)
    for step_index in range(2):
        column_total, drawdown = column_data[step_index]
        water_slope, oil_slope = mobility_slopes(
            saturation[step_index + 1, 0][column_x, column_y],
            saturation[step_index + 1, 1][column_x, column_y],
        )
        weight = misfit[step_index][:, None] * column_perm * perforated
        added = jnp.stack(
            [weight * column_total, weight * drawdown * water_slope, weight * drawdown * oil_slope]
        )
        sources.append(
            jnp.zeros((3,) + permeability.shape, jnp.float32).at[:, column_x, column_y].add(added)
        )
        explicit = explicit.at[column_x, column_y].add(weight * column_total * drawdown)
    sources[1] = sources[1].at[1].add(saturation[2, 0] - seismic_obs)

    def solve(step_index, source):
        lagrange = apply_inverse(diag_inverse[step_index], source)
        for sweep_index in range(ITERS - 1):
            upper_terms, lower_terms, spare_leading, unused_behind = neighbour_terms(
                lagrange, ahead_coef[step_index], behind_coef[step_index], False
            )
            face_total = (
                upper_terms[0]
                + lower_terms[0]
                + upper_terms[1]
                + lower_terms[1]
                + upper_terms[2]
                + lower_terms[2]
            )
            coupling = face_total + fault_sum(lagrange, fault_coef[step_index], cell_index)
            residual = jnp.concatenate([(source[0] + coupling)[None], source[1:]], axis=0)
            lagrange = apply_inverse(diag_inverse[step_index], residual)
        return lagrange

    late = solve(1, sources[1])
    early_source = sources[0] + jnp.stack(
        [jnp.zeros_like(porosity), porosity * (late[0] - late[2]), porosity * (late[1] - late[2])]
    )
    early = solve(0, early_source)
    solved = [early, late]
    flux_list = []
    porosity_terms = []
    for step_index in (1, 0):
        lagrange = solved[step_index]
        upper_terms, lower_terms, local_ahead, local_behind = neighbour_terms(
            lagrange, ahead_coef[step_index], behind_coef[step_index], True
        )
        pressure_here = pressure[step_index]
        flux_grad = jnp.zeros_like(pressure_here)
        for direction in range(3):
            flux_grad = (
                flux_grad
                + 0.5
                * (pressure_here - pressure_ahead[step_index][direction])
                * (local_ahead[direction] - upper_terms[direction])
                + 0.5
                * (pressure_trailing[step_index][direction] - pressure_here)
                * (lower_terms[direction] - local_behind[direction])
            )
        flux_list.append(flux_grad)
        water_change = saturation[step_index + 1, 0] - saturation[step_index, 0]
        oil_change = saturation[step_index + 1, 1] - saturation[step_index, 1]
        porosity_terms.append(
            lagrange[0] * water_change
            + lagrange[1] * oil_change
            - lagrange[2] * (water_change + oil_change)
        )
    log_perm_grad = explicit - (flux_list[0] + flux_list[1])
    porosity_gradient = -(porosity_terms[0] + porosity_terms[1])
    box_totals = jnp.stack([box_sums(log_perm_grad), box_sums(porosity_gradient)], axis=1)
    region_labels = PARAM_REGIONS * lax.axis_size("gx") * lax.axis_size("gy") * lax.axis_size("gz")
    region_partial = jax.ops.segment_sum(
        box_totals, region_map.reshape(-1), num_segments=region_labels
    ).T
    region_grad = lax.psum_scatter(
        region_partial, ("gx", "gy", "gz"), scatter_dimension=1, tiled=True
    )
    return (jnp.stack([early, late]), region_grad)


def solution(mesh):
    placed = (
        P(None, "gx", "gy", "gz"),
        P(None, None, "gx", "gy", "gz"),
        P("gx", "gy", "gz"),
        P("gx", "gy", "gz"),
        P("gx", "gy", "gz"),
        P(None, None, None, "gx", "gy", "gz"),
        P("gx", "gy", "gz"),
        P("gx", "gy", None),
        P("gx", "gy", None),
        P("gx", "gy", None),
        P("gx", "gy", None),
        P(None, "gx", "gy", None),
        P(None, "gx", "gy", None),
        P(("gx", "gy", "gz"), None, None),
        P(("gx", "gy", "gz"), None),
        P(("gx", "gy", "gz"), None, None),
        P(("gx", "gy", "gz"), None, None),
        P("gx", "gy", "gz"),
    )
    return jax.shard_map(
        local,
        mesh=mesh,
        in_specs=placed,
        out_specs=(P(None, None, "gx", "gy", "gz"), P(None, ("gx", "gy", "gz"))),
        check_vma=False,
    )
```

profile of v0, /device:TPU:0, one launch (start us, length us, event | category | flops | bytes accessed | tf_op | source)
XLA Modules:
  0.0 1039.0 jit_solution(6294457973169037684)
XLA Ops:
  18.0 8.5 psum.7
  40.4 11.0 %gather_fusion.8 = f32[2048,3]{1,0:T(8,128)} fusion(f32[3,16384]{0,1:T(8,128)} %bitcast.380, s32[2048]{0:T(1024)S(1)} %fusion.262), kind=kCustom, calls=%fused_computation.8 | custom fusion | bytes 57344 | tf_op jit(solution)/shard_map/gather | solution.py:68
  83.9 11.0 %gather_fusion.7 = f32[2048,6]{1,0:T(8,128)} fusion(f32[6,16384]{0,1:T(8,128)} %copy.142, s32[2048]{0:T(1024)S(1)} %fusion.262), kind=kCustom, calls=%fused_computation.7 | custom fusion | bytes 106496 | tf_op jit(solution)/shard_map/gather | solution.py:172
  123.1 12.0 %scatter_custom_fusion.1 = f32[16384]{0:T(1024)} fusion(s32[2048]{0:T(1024)} %bitcast.453, f32[2048]{0:T(1024)S(1)} %bitcast.444, f32[]{:T(128)} %constant.81.clone.1), kind=kCustom, calls=%fused_computation.698 | custom fusion | flops 2048 | bytes 66048 | tf_op jit(solution)/shard_map/scatter-add | solution.py:74
  180.3 11.0 %gather_fusion.9 = f32[2048,3]{1,0:T(8,128)} fusion(f32[3,16384]{0,1:T(8,128)} %bitcast.383, s32[2048]{0:T(1024)S(1)} %fusion.262), kind=kCustom, calls=%fused_computation.9 | custom fusion | bytes 57344 | tf_op jit(solution)/shard_map/gather | solution.py:68
  207.4 12.0 %scatter_custom_fusion.2 = f32[16384]{0:T(1024)} fusion(s32[2048]{0:T(1024)} %bitcast.454, f32[2048]{0:T(1024)S(1)} %bitcast.447, f32[]{:T(128)} %constant.81.clone.1), kind=kCustom, calls=%fused_computation.696 | custom fusion | flops 2048 | bytes 66048 | tf_op jit(solution)/shard_map/scatter-add | solution.py:74
  241.6 11.0 %gather_fusion.10 = f32[2048,3]{1,0:T(8,128)} fusion(f32[3,16384]{0,1:T(8,128)} %bitcast.384, s32[2048]{0:T(1024)S(1)} %fusion.262), kind=kCustom, calls=%fused_computation.10 | custom fusion | bytes 57344 | tf_op jit(solution)/shard_map/gather | solution.py:68
  254.7 11.1 %all-to-all-start.3 = ((f32[3,16,128]{2,0,1:T(4,128)}), f32[3,16,128]{2,0,1:T(4,128)}, u32[]{:S(2)}, u32[]{:S(2)}) async-start(f32[3,16,128]{2,0,1:T(4,128)} %bitcast.436), calls=%async_computation.3 | async-start | bytes 65536 | tf_op jit(solution)/shard_map/all_to_all | solution.py:63
  275.6 12.0 %scatter_custom_fusion.3 = f32[16384]{0:T(1024)} fusion(s32[2048]{0:T(1024)} %bitcast.455, f32[2048]{0:T(1024)S(1)} %bitcast.448, f32[]{:T(128)} %constant.81.clone.1), kind=kCustom, calls=%fused_computation.694 | custom fusion | flops 2048 | bytes 66048 | tf_op jit(solution)/shard_map/scatter-add | solution.py:74
  310.0 11.0 %gather_fusion.11 = f32[2048,3]{1,0:T(8,128)} fusion(f32[3,16384]{0,1:T(8,128)} %bitcast.385, s32[2048]{0:T(1024)S(1)} %fusion.262), kind=kCustom, calls=%fused_computation.11 | custom fusion | bytes 57344 | tf_op jit(solution)/shard_map/gather | solution.py:68
  323.1 11.2 %all-to-all-start.4 = ((f32[3,16,128]{2,0,1:T(4,128)}), f32[3,16,128]{2,0,1:T(4,128)}, u32[]{:S(2)}, u32[]{:S(2)}) async-start(f32[3,16,128]{2,0,1:T(4,128)} %bitcast.437), calls=%async_computation.4 | async-start | bytes 65536 | tf_op jit(solution)/shard_map/all_to_all | solution.py:63
  344.1 12.0 %scatter_custom_fusion.4 = f32[16384]{0:T(1024)} fusion(s32[2048]{0:T(1024)} %bitcast.456, f32[2048]{0:T(1024)S(1)} %bitcast.449, f32[]{:T(128)} %constant.81.clone.1), kind=kCustom, calls=%fused_computation.692 | custom fusion | flops 2048 | bytes 66048 | tf_op jit(solution)/shard_map/scatter-add | solution.py:74
  414.9 11.0 %gather_fusion.12 = f32[2048,3]{1,0:T(8,128)} fusion(f32[3,16384]{0,1:T(8,128)} %bitcast.386, s32[2048]{0:T(1024)S(1)} %fusion.262), kind=kCustom, calls=%fused_computation.12 | custom fusion | bytes 57344 | tf_op jit(solution)/shard_map/gather | solution.py:68
  428.0 11.1 %all-to-all-start.5 = ((f32[3,16,128]{2,0,1:T(4,128)}), f32[3,16,128]{2,0,1:T(4,128)}, u32[]{:S(2)}, u32[]{:S(2)}) async-start(f32[3,16,128]{2,0,1:T(4,128)} %bitcast.438), calls=%async_computation.5 | async-start | bytes 65536 | tf_op jit(solution)/shard_map/all_to_all | solution.py:63
  449.0 12.0 %scatter_custom_fusion.5 = f32[16384]{0:T(1024)} fusion(s32[2048]{0:T(1024)} %bitcast.457, f32[2048]{0:T(1024)S(1)} %bitcast.446, f32[]{:T(128)} %constant.81.clone.1), kind=kCustom, calls=%fused_computation.690 | custom fusion | flops 2048 | bytes 66048 | tf_op jit(solution)/shard_map/scatter-add | solution.py:74
  496.7 11.0 %gather_fusion.15 = f32[2048,3]{1,0:T(8,128)} fusion(f32[3,16384]{0,1:T(8,128)} %bitcast.381, s32[2048]{0:T(1024)S(1)} %fusion.262), kind=kCustom, calls=%fused_computation.15 | custom fusion | bytes 57344 | tf_op jit(solution)/shard_map/gather | solution.py:68
  509.8 11.2 %all-to-all-start.6 = ((f32[3,16,128]{2,0,1:T(4,128)}), f32[3,16,128]{2,0,1:T(4,128)}, u32[]{:S(2)}, u32[]{:S(2)}) async-start(f32[3,16,128]{2,0,1:T(4,128)} %bitcast.434), calls=%async_computation.6 | async-start | bytes 65536 | tf_op jit(solution)/shard_map/all_to_all | solution.py:63
  531.5 12.0 %scatter_custom_fusion.7 = f32[16384]{0:T(1024)} fusion(s32[2048]{0:T(1024)} %bitcast.458, f32[2048]{0:T(1024)S(1)} %bitcast.443, f32[]{:T(128)} %constant.81.clone.1), kind=kCustom, calls=%fused_computation.688 | custom fusion | flops 2048 | bytes 66048 | tf_op jit(solution)/shard_map/scatter-add | solution.py:74
  565.5 11.0 %gather_fusion.16 = f32[2048,3]{1,0:T(8,128)} fusion(f32[3,16384]{0,1:T(8,128)} %bitcast.387, s32[2048]{0:T(1024)S(1)} %fusion.262), kind=kCustom, calls=%fused_computation.16 | custom fusion | bytes 57344 | tf_op jit(solution)/shard_map/gather | solution.py:68
  578.6 11.4 %all-to-all-start.7 = ((f32[3,16,128]{2,0,1:T(4,128)}), f32[3,16,128]{2,0,1:T(4,128)}, u32[]{:S(2)}, u32[]{:S(2)}) async-start(f32[3,16,128]{2,0,1:T(4,128)} %bitcast.113), calls=%async_computation.7 | async-start | bytes 65536 | tf_op jit(solution)/shard_map/all_to_all | solution.py:63
  598.2 11.4 %scatter_custom_fusion.8 = f32[16384]{0:T(1024)S(1)} fusion(s32[2048]{0:T(1024)} %bitcast.459, f32[2048]{0:T(1024)S(1)} %bitcast.450, f32[]{:T(128)} %constant.81.clone.1), kind=kCustom, calls=%fused_computation.686 | custom fusion | flops 2048 | bytes 66048 | tf_op jit(solution)/shard_map/scatter-add | solution.py:74
  654.1 10.9 %gather_fusion.17 = f32[2048,3]{1,0:T(8,128)} fusion(f32[3,16384]{0,1:T(8,128)} %bitcast.388, s32[2048]{0:T(1024)S(1)} %fusion.262), kind=kCustom, calls=%fused_computation.17 | custom fusion | bytes 57344 | tf_op jit(solution)/shard_map/gather | solution.py:68
  667.2 10.7 %all-to-all-start.8 = ((f32[3,16,128]{2,0,1:T(4,128)}), f32[3,16,128]{2,0,1:T(4,128)}, u32[]{:S(2)}, u32[]{:S(2)}) async-start(f32[3,16,128]{2,0,1:T(4,128)} %bitcast.439), calls=%async_computation.8 | async-start | bytes 65536 | tf_op jit(solution)/shard_map/all_to_all | solution.py:63
  685.9 11.4 %scatter_custom_fusion.9 = f32[16384]{0:T(1024)S(1)} fusion(s32[2048]{0:T(1024)} %bitcast.460, f32[2048]{0:T(1024)S(1)} %bitcast.451, f32[]{:T(128)} %constant.81.clone.1), kind=kCustom, calls=%fused_computation.684 | custom fusion | flops 2048 | bytes 66048 | tf_op jit(solution)/shard_map/scatter-add | solution.py:74
  725.9 10.9 %gather_fusion.18 = f32[2048,3]{1,0:T(8,128)} fusion(f32[3,16384]{0,1:T(8,128)} %bitcast.389, s32[2048]{0:T(1024)S(1)} %fusion.262), kind=kCustom, calls=%fused_computation.18 | custom fusion | bytes 57344 | tf_op jit(solution)/shard_map/gather | solution.py:68
  738.9 7.9 all-to-all-start.9
  755.7 12.0 %scatter_custom_fusion.10 = f32[16384]{0:T(1024)} fusion(s32[2048]{0:T(1024)} %bitcast.461, f32[2048]{0:T(1024)S(1)} %bitcast.452, f32[]{:T(128)} %constant.81.clone.1), kind=kCustom, calls=%fused_computation.682 | custom fusion | flops 2048 | bytes 66048 | tf_op jit(solution)/shard_map/scatter-add | solution.py:74
  792.7 10.9 %gather_fusion.19 = f32[2048,3]{1,0:T(8,128)} fusion(f32[3,16384]{0,1:T(8,128)} %bitcast.382, s32[2048]{0:T(1024)S(1)} %fusion.262), kind=kCustom, calls=%fused_computation.19 | custom fusion | bytes 57344 | tf_op jit(solution)/shard_map/gather | solution.py:68
  805.8 11.2 %all-to-all-start.10 = ((f32[3,16,128]{2,0,1:T(4,128)}), f32[3,16,128]{2,0,1:T(4,128)S(1)}, u32[]{:S(2)}, u32[]{:S(2)}) async-start(f32[3,16,128]{2,0,1:T(4,128)} %bitcast.131), calls=%async_computation.10 | async-start | bytes 65536 | tf_op jit(solution)/shard_map/all_to_all | solution.py:63
  825.3 11.4 %scatter_custom_fusion.11 = f32[16384]{0:T(1024)S(1)} fusion(s32[2048]{0:T(1024)} %bitcast.462, f32[2048]{0:T(1024)S(1)} %bitcast.445, f32[]{:T(128)} %constant.81.clone.1), kind=kCustom, calls=%fused_computation.680 | custom fusion | flops 2048 | bytes 66048 | tf_op jit(solution)/shard_map/scatter-add | solution.py:74
  860.2 9.6 add_reduce_fusion
  889.7 141.0 %reduce-scatter.2.cloned.1.call-done = f32[2,32]{0,1:T(8,128)} async-done(((f32[2,1024]{0,1:T(8,128)}), f32[2,32]{0,1:T(8,128)}) %reduce-scatter.2.cloned.1.call-update) | async-done | bytes 272 | tf_op jit(solution)/shard_map/reduce_scatter | solution.py:282
  (721 shorter events, 538.0 us)
Async XLA Ops:
  53.6 55.2 %all-to-all-start.1 = ((f32[3,16,128]{2,0,1:T(4,128)}), f32[3,16,128]{2,0,1:T(4,128)S(1)}, u32[]{:S(2)}, u32[]{:S(2)}) async-start(f32[3,16,128]{2,0,1:T(4,128)} %bitcast.61), calls=%async_computation.1 | async-start | bytes 65536 | tf_op jit(solution)/shard_map/all_to_all | solution.py:63
  58.7 44.7 %collective-permute-start = (f32[10,1,8,128]{3,2,1,0:T(8,128)S(1)}, f32[10,1,8,128]{3,2,1,0:T(8,128)S(1)}, u32[]{:S(2)}, u32[]{:S(2)}) collective-permute-start(f32[10,1,8,128]{3,2,1,0:T(8,128)S(1)} %get-tuple-element.154), channel_id=1, source_target_pairs={{0,16},{1,17},{2,18},{3,19},{4,20},{5,21},{6,22},{7,23},{8,24},{9,... | collective-permute-start | bytes 122888 | tf_op jit(solution)/shard_map/ppermute | solution.py:18
  62.1 41.3 %collective-permute-start.1 = (f32[10,1,8,128]{3,2,1,0:T(8,128)S(1)}, f32[10,1,8,128]{3,2,1,0:T(8,128)S(1)}, u32[]{:S(2)}, u32[]{:S(2)}) collective-permute-start(f32[10,1,8,128]{3,2,1,0:T(8,128)S(1)} %get-tuple-element.155), channel_id=1, source_target_pairs={{16,0},{17,1},{18,2},{19,3},{20,4},{21,5},{22,6},{23,7},{24,8},{25... | collective-permute-start | bytes 122888 | tf_op jit(solution)/shard_map/ppermute | solution.py:21
  71.3 25.7 %collective-permute-start.6 = (f32[3,18,1,128]{3,2,1,0:T(1,128)}, f32[3,18,1,128]{3,2,1,0:T(1,128)S(1)}, u32[]{:S(2)}, u32[]{:S(2)}) collective-permute-start(f32[3,18,1,128]{3,2,1,0:T(1,128)} %get-tuple-element.227), channel_id=1, source_target_pairs={{4,0},{8,4},{12,8},{5,1},{9,5},{13,9},{6,2},{10,6},{14,10},{7,3},{... | collective-permute-start | bytes 82952 | tf_op jit(solution)/shard_map/ppermute | solution.py:21
  98.1 59.0 %collective-permute-start.10 = (f32[3,18,10,1]{3,2,1,0:T(8,128)}, f32[3,18,10,1]{3,2,1,0:T(8,128)}, u32[]{:S(2)}, u32[]{:S(2)}) collective-permute-start(f32[3,18,10,1]{3,2,1,0:T(8,128)} %get-tuple-element.179), channel_id=1, source_target_pairs={{1,0},{2,1},{3,2},{5,4},{6,5},{7,6},{9,8},{10,9},{11,10},{13,12},{... | collective-permute-start | bytes 6488 | tf_op jit(solution)/shard_map/ppermute | solution.py:21
  99.6 57.6 %collective-permute-start.11 = (f32[3,18,10,1]{3,2,1,0:T(8,128)}, f32[3,18,10,1]{3,2,1,0:T(8,128)}, u32[]{:S(2)}, u32[]{:S(2)}) collective-permute-start(f32[3,18,10,1]{3,2,1,0:T(8,128)} %get-tuple-element.178), channel_id=1, source_target_pairs={{0,1},{1,2},{2,3},{4,5},{5,6},{6,7},{8,9},{9,10},{10,11},{12,13},{... | collective-permute-start | bytes 6488 | tf_op jit(solution)/shard_map/ppermute | solution.py:18
  103.5 31.5 %collective-permute-start.4 = (f32[10,18,1,128]{3,2,1,0:T(1,128)S(1)}, f32[10,18,1,128]{3,2,1,0:T(1,128)S(1)}, u32[]{:S(2)}, u32[]{:S(2)}) collective-permute-start(f32[10,18,1,128]{3,2,1,0:T(1,128)S(1)} %get-tuple-element.152), channel_id=1, source_target_pairs={{0,4},{4,8},{8,12},{1,5},{5,9},{9,13},{2,6},{6,10},{10,14},{3,7},{... | collective-permute-start | bytes 276488 | tf_op jit(solution)/shard_map/ppermute | solution.py:18
  107.4 27.8 %collective-permute-start.5 = (f32[10,18,1,128]{3,2,1,0:T(1,128)S(1)}, f32[10,18,1,128]{3,2,1,0:T(1,128)S(1)}, u32[]{:S(2)}, u32[]{:S(2)}) collective-permute-start(f32[10,18,1,128]{3,2,1,0:T(1,128)S(1)} %get-tuple-element.153), channel_id=1, source_target_pairs={{4,0},{8,4},{12,8},{5,1},{9,5},{13,9},{6,2},{10,6},{14,10},{7,3},{... | collective-permute-start | bytes 276488 | tf_op jit(solution)/shard_map/ppermute | solution.py:21
  168.3 29.4 %collective-permute-start.14 = (f32[3,18,1,128]{3,2,1,0:T(1,128)}, f32[3,18,1,128]{3,2,1,0:T(1,128)}, u32[]{:S(2)}, u32[]{:S(2)}) collective-permute-start(f32[3,18,1,128]{3,2,1,0:T(1,128)} %get-tuple-element.225), channel_id=1, source_target_pairs={{4,0},{8,4},{12,8},{5,1},{9,5},{13,9},{6,2},{10,6},{14,10},{7,3},{... | collective-permute-start | bytes 82952 | tf_op jit(solution)/shard_map/ppermute | solution.py:21
  169.6 28.1 %collective-permute-start.15 = (f32[3,18,1,128]{3,2,1,0:T(1,128)}, f32[3,18,1,128]{3,2,1,0:T(1,128)}, u32[]{:S(2)}, u32[]{:S(2)}) collective-permute-start(f32[3,18,1,128]{3,2,1,0:T(1,128)} %get-tuple-element.224), channel_id=1, source_target_pairs={{0,4},{4,8},{8,12},{1,5},{5,9},{9,13},{2,6},{6,10},{10,14},{3,7},{... | collective-permute-start | bytes 82952 | tf_op jit(solution)/shard_map/ppermute | solution.py:18
  229.5 36.4 %collective-permute-start.20 = (f32[3,18,1,128]{3,2,1,0:T(1,128)}, f32[3,18,1,128]{3,2,1,0:T(1,128)}, u32[]{:S(2)}, u32[]{:S(2)}) collective-permute-start(f32[3,18,1,128]{3,2,1,0:T(1,128)} %get-tuple-element.223), channel_id=1, source_target_pairs={{4,0},{8,4},{12,8},{5,1},{9,5},{13,9},{6,2},{10,6},{14,10},{7,3},{... | collective-permute-start | bytes 82952 | tf_op jit(solution)/shard_map/ppermute | solution.py:21
  230.8 35.1 %collective-permute-start.21 = (f32[3,18,1,128]{3,2,1,0:T(1,128)}, f32[3,18,1,128]{3,2,1,0:T(1,128)}, u32[]{:S(2)}, u32[]{:S(2)}) collective-permute-start(f32[3,18,1,128]{3,2,1,0:T(1,128)} %get-tuple-element.222), channel_id=1, source_target_pairs={{0,4},{4,8},{8,12},{1,5},{5,9},{9,13},{2,6},{6,10},{10,14},{3,7},{... | collective-permute-start | bytes 82952 | tf_op jit(solution)/shard_map/ppermute | solution.py:18
  297.7 36.6 %collective-permute-start.26 = (f32[3,18,1,128]{3,2,1,0:T(1,128)}, f32[3,18,1,128]{3,2,1,0:T(1,128)}, u32[]{:S(2)}, u32[]{:S(2)}) collective-permute-start(f32[3,18,1,128]{3,2,1,0:T(1,128)} %get-tuple-element.221), channel_id=1, source_target_pairs={{4,0},{8,4},{12,8},{5,1},{9,5},{13,9},{6,2},{10,6},{14,10},{7,3},{... | collective-permute-start | bytes 82952 | tf_op jit(solution)/shard_map/ppermute | solution.py:21
  299.0 35.4 %collective-permute-start.27 = (f32[3,18,1,128]{3,2,1,0:T(1,128)}, f32[3,18,1,128]{3,2,1,0:T(1,128)}, u32[]{:S(2)}, u32[]{:S(2)}) collective-permute-start(f32[3,18,1,128]{3,2,1,0:T(1,128)} %get-tuple-element.220), channel_id=1, source_target_pairs={{0,4},{4,8},{8,12},{1,5},{5,9},{9,13},{2,6},{6,10},{10,14},{3,7},{... | collective-permute-start | bytes 82952 | tf_op jit(solution)/shard_map/ppermute | solution.py:18
  366.3 72.9 %collective-permute-start.32 = (f32[3,18,1,128]{3,2,1,0:T(1,128)}, f32[3,18,1,128]{3,2,1,0:T(1,128)}, u32[]{:S(2)}, u32[]{:S(2)}) collective-permute-start(f32[3,18,1,128]{3,2,1,0:T(1,128)} %get-tuple-element.219), channel_id=1, source_target_pairs={{4,0},{8,4},{12,8},{5,1},{9,5},{13,9},{6,2},{10,6},{14,10},{7,3},{... | collective-permute-start | bytes 82952 | tf_op jit(solution)/shard_map/ppermute | solution.py:21
  367.6 71.6 %collective-permute-start.33 = (f32[3,18,1,128]{3,2,1,0:T(1,128)}, f32[3,18,1,128]{3,2,1,0:T(1,128)}, u32[]{:S(2)}, u32[]{:S(2)}) collective-permute-start(f32[3,18,1,128]{3,2,1,0:T(1,128)} %get-tuple-element.218), channel_id=1, source_target_pairs={{0,4},{4,8},{8,12},{1,5},{5,9},{9,13},{2,6},{6,10},{10,14},{3,7},{... | collective-permute-start | bytes 82952 | tf_op jit(solution)/shard_map/ppermute | solution.py:18
  481.8 39.2 %collective-permute-start.38 = (f32[3,18,1,128]{3,2,1,0:T(1,128)}, f32[3,18,1,128]{3,2,1,0:T(1,128)}, u32[]{:S(2)}, u32[]{:S(2)}) collective-permute-start(f32[3,18,1,128]{3,2,1,0:T(1,128)} %get-tuple-element.217), channel_id=1, source_target_pairs={{4,0},{8,4},{12,8},{5,1},{9,5},{13,9},{6,2},{10,6},{14,10},{7,3},{... | collective-permute-start | bytes 82952 | tf_op jit(solution)/shard_map/ppermute | solution.py:21
  483.1 37.9 %collective-permute-start.39 = (f32[3,18,1,128]{3,2,1,0:T(1,128)}, f32[3,18,1,128]{3,2,1,0:T(1,128)}, u32[]{:S(2)}, u32[]{:S(2)}) collective-permute-start(f32[3,18,1,128]{3,2,1,0:T(1,128)} %get-tuple-element.216), channel_id=1, source_target_pairs={{0,4},{4,8},{8,12},{1,5},{5,9},{9,13},{2,6},{6,10},{10,14},{3,7},{... | collective-permute-start | bytes 82952 | tf_op jit(solution)/shard_map/ppermute | solution.py:18
  553.2 36.8 %collective-permute-start.44 = (f32[3,18,1,128]{3,2,1,0:T(1,128)S(1)}, f32[3,18,1,128]{3,2,1,0:T(1,128)S(1)}, u32[]{:S(2)}, u32[]{:S(2)}) collective-permute-start(f32[3,18,1,128]{3,2,1,0:T(1,128)S(1)} %get-tuple-element.215), channel_id=1, source_target_pairs={{4,0},{8,4},{12,8},{5,1},{9,5},{13,9},{6,2},{10,6},{14,10},{7,3},{... | collective-permute-start | bytes 82952 | tf_op jit(solution)/shard_map/ppermute | solution.py:21
  554.5 35.5 %collective-permute-start.45 = (f32[3,18,1,128]{3,2,1,0:T(1,128)S(1)}, f32[3,18,1,128]{3,2,1,0:T(1,128)S(1)}, u32[]{:S(2)}, u32[]{:S(2)}) collective-permute-start(f32[3,18,1,128]{3,2,1,0:T(1,128)S(1)} %get-tuple-element.214), channel_id=1, source_target_pairs={{0,4},{4,8},{8,12},{1,5},{5,9},{9,13},{2,6},{6,10},{10,14},{3,7},{... | collective-permute-start | bytes 82952 | tf_op jit(solution)/shard_map/ppermute | solution.py:18
  617.4 24.9 %collective-permute-start.66 = (f32[3,1,8,128]{3,2,1,0:T(8,128)S(1)}, f32[3,1,8,128]{3,2,1,0:T(8,128)S(1)}, u32[]{:S(2)}, u32[]{:S(2)}) collective-permute-start(f32[3,1,8,128]{3,2,1,0:T(8,128)S(1)} %get-tuple-element.229), channel_id=1, source_target_pairs={{16,0},{17,1},{18,2},{19,3},{20,4},{21,5},{22,6},{23,7},{24,8},{25... | collective-permute-start | bytes 36872 | tf_op jit(solution)/shard_map/ppermute | solution.py:21
  636.5 41.3 %collective-permute-start.50 = (f32[3,18,1,128]{3,2,1,0:T(1,128)}, f32[3,18,1,128]{3,2,1,0:T(1,128)S(1)}, u32[]{:S(2)}, u32[]{:S(2)}) collective-permute-start(f32[3,18,1,128]{3,2,1,0:T(1,128)} %get-tuple-element.213), channel_id=1, source_target_pairs={{4,0},{8,4},{12,8},{5,1},{9,5},{13,9},{6,2},{10,6},{14,10},{7,3},{... | collective-permute-start | bytes 82952 | tf_op jit(solution)/shard_map/ppermute | solution.py:21
  637.8 40.1 %collective-permute-start.51 = (f32[3,18,1,128]{3,2,1,0:T(1,128)}, f32[3,18,1,128]{3,2,1,0:T(1,128)S(1)}, u32[]{:S(2)}, u32[]{:S(2)}) collective-permute-start(f32[3,18,1,128]{3,2,1,0:T(1,128)} %get-tuple-element.212), channel_id=1, source_target_pairs={{0,4},{4,8},{8,12},{1,5},{5,9},{9,13},{2,6},{6,10},{10,14},{3,7},{... | collective-permute-start | bytes 82952 | tf_op jit(solution)/shard_map/ppermute | solution.py:18
  643.0 61.4 %collective-permute-start.68 = (f32[3,18,1,128]{3,2,1,0:T(1,128)}, f32[3,18,1,128]{3,2,1,0:T(1,128)S(1)}, u32[]{:S(2)}, u32[]{:S(2)}) collective-permute-start(f32[3,18,1,128]{3,2,1,0:T(1,128)} %get-tuple-element.201), channel_id=1, source_target_pairs={{4,0},{8,4},{12,8},{5,1},{9,5},{13,9},{6,2},{10,6},{14,10},{7,3},{... | collective-permute-start | bytes 82952 | tf_op jit(solution)/shard_map/ppermute | solution.py:21
  644.3 60.2 %collective-permute-start.69 = (f32[3,18,1,128]{3,2,1,0:T(1,128)}, f32[3,18,1,128]{3,2,1,0:T(1,128)}, u32[]{:S(2)}, u32[]{:S(2)}) collective-permute-start(f32[3,18,1,128]{3,2,1,0:T(1,128)} %get-tuple-element.200), channel_id=1, source_target_pairs={{0,4},{4,8},{8,12},{1,5},{5,9},{9,13},{2,6},{6,10},{10,14},{3,7},{... | collective-permute-start | bytes 82952 | tf_op jit(solution)/shard_map/ppermute | solution.py:18
  705.9 41.0 %collective-permute-start.56 = (f32[3,18,1,128]{3,2,1,0:T(1,128)S(1)}, f32[3,18,1,128]{3,2,1,0:T(1,128)S(1)}, u32[]{:S(2)}, u32[]{:S(2)}) collective-permute-start(f32[3,18,1,128]{3,2,1,0:T(1,128)S(1)} %get-tuple-element.211), channel_id=1, source_target_pairs={{4,0},{8,4},{12,8},{5,1},{9,5},{13,9},{6,2},{10,6},{14,10},{7,3},{... | collective-permute-start | bytes 82952 | tf_op jit(solution)/shard_map/ppermute | solution.py:21
  707.2 39.7 %collective-permute-start.57 = (f32[3,18,1,128]{3,2,1,0:T(1,128)S(1)}, f32[3,18,1,128]{3,2,1,0:T(1,128)S(1)}, u32[]{:S(2)}, u32[]{:S(2)}) collective-permute-start(f32[3,18,1,128]{3,2,1,0:T(1,128)S(1)} %get-tuple-element.210), channel_id=1, source_target_pairs={{0,4},{4,8},{8,12},{1,5},{5,9},{9,13},{2,6},{6,10},{10,14},{3,7},{... | collective-permute-start | bytes 82952 | tf_op jit(solution)/shard_map/ppermute | solution.py:18
  712.8 72.0 %collective-permute-start.70 = (f32[3,18,10,1]{3,2,1,0:T(8,128)}, f32[3,18,10,1]{3,2,1,0:T(8,128)}, u32[]{:S(2)}, u32[]{:S(2)}) collective-permute-start(f32[3,18,10,1]{3,2,1,0:T(8,128)} %get-tuple-element.157), channel_id=1, source_target_pairs={{1,0},{2,1},{3,2},{5,4},{6,5},{7,6},{9,8},{10,9},{11,10},{13,12},{... | collective-permute-start | bytes 6488 | tf_op jit(solution)/shard_map/ppermute | solution.py:21
  714.1 70.7 %collective-permute-start.71 = (f32[3,18,10,1]{3,2,1,0:T(8,128)}, f32[3,18,10,1]{3,2,1,0:T(8,128)}, u32[]{:S(2)}, u32[]{:S(2)}) collective-permute-start(f32[3,18,10,1]{3,2,1,0:T(8,128)} %get-tuple-element.156), channel_id=1, source_target_pairs={{0,1},{1,2},{2,3},{4,5},{5,6},{6,7},{8,9},{9,10},{10,11},{12,13},{... | collective-permute-start | bytes 6488 | tf_op jit(solution)/shard_map/ppermute | solution.py:18
  778.2 38.8 %collective-permute-start.62 = (f32[3,18,1,128]{3,2,1,0:T(1,128)}, f32[3,18,1,128]{3,2,1,0:T(1,128)}, u32[]{:S(2)}, u32[]{:S(2)}) collective-permute-start(f32[3,18,1,128]{3,2,1,0:T(1,128)} %get-tuple-element.209), channel_id=1, source_target_pairs={{4,0},{8,4},{12,8},{5,1},{9,5},{13,9},{6,2},{10,6},{14,10},{7,3},{... | collective-permute-start | bytes 82952 | tf_op jit(solution)/shard_map/ppermute | solution.py:21
  779.7 37.4 %collective-permute-start.63 = (f32[3,18,1,128]{3,2,1,0:T(1,128)}, f32[3,18,1,128]{3,2,1,0:T(1,128)}, u32[]{:S(2)}, u32[]{:S(2)}) collective-permute-start(f32[3,18,1,128]{3,2,1,0:T(1,128)} %get-tuple-element.208), channel_id=1, source_target_pairs={{0,4},{4,8},{8,12},{1,5},{5,9},{9,13},{2,6},{6,10},{10,14},{3,7},{... | collective-permute-start | bytes 82952 | tf_op jit(solution)/shard_map/ppermute | solution.py:18
  817.0 213.6 %reduce-scatter.2.cloned.1.call-start = ((), (), s32[]{:S(2)}) async-start(), calls=%async_computation.12 | async-start | bytes 540672 | tf_op jit(solution)/shard_map/reduce_scatter | solution.py:282
  (201 other events, 2321.9 us)
Sparse Core Ops, SparseCore 0:
  889.0 141.5 reduce-scatter.1
where the time goes:
time: 1060 us; the launch traced here: 1040 us
  starting transfers between devices  321 us (30%)
  local copies, waits for them, and re-layouts  285 us (27%)
  other arithmetic  245 us (23%)
  waiting for transfers between devices  161 us (15%)
  between operations  17.7 us (2%)
    ppermute x39, starting transfers between devices, extended_2(): lax.ppermute(lax.slice_in_dim(block, block.shape[dim] - width, None, axis...  169 us
    reduce_scatter x1, waiting for transfers between devices, local(): lax.psum_scatter(region_partial, ('gx', 'gy', 'gz'), scatter_dimension=1,...  141 us
    gather x20, local copies, waits for them, and re-layouts, fault_sum(): own_values = flattened[:, cell_index]  131 us
    scatter-add x10, other arithmetic, fault_sum(): faults = jnp.zeros((flattened.shape[1],), jnp.float32).at[cell_index.resh...  118 us
    all_to_all x10, starting transfers between devices, fault_exchange(): lax.all_to_all(values, ('gy', 'gz'), split_axis=1, concat_axis=1, tiled=T...  94.9 us
    reshape x10, local copies, waits for them, and re-layouts, fault_sum(): flattened = lagrange.reshape(lagrange.shape[0], -1)  53.4 us
    ppermute x39, starting transfers between devices, extended_2(): lax.ppermute(lax.slice_in_dim(block, 0, width, axis=dim), axis, backward)  51.4 us
  transfers between devices with their start and end apart: 90, of which 19 were waited for; matrix products, arithmetic and copies ran while one was open for 35% of the time, Pallas kernels for 0%

commit v1 on v0

--- a/solution.py
+++ b/solution.py
@@ -60,7 +60,12 @@
 
 
 def fault_exchange(values):
-    return lax.all_to_all(values, ("gy", "gz"), split_axis=1, concat_axis=1, tiled=True)
+    return jnp.concatenate(
+        lax.all_to_all(
+            jnp.stack(jnp.split(values, lax.axis_size(("gy", "gz")), axis=1)), ("gy", "gz"), 0, 0
+        ),
+        axis=1,
+    )
 
 
 def fault_sum(lagrange, coefficient, cell_index):

time: 1060 us -> 1080 us (1.019)
  local copies, waits for them, and re-layouts: 285 us -> 358 us
  other arithmetic: 245 us -> 203 us
    unnamed x288 -> x378, local copies, waits for them, and re-layouts: 4.35 us -> 90.8 us
  transfers between devices with their start and end apart: 90 -> 90, of which waited for: 19 -> 21; matrix products, arithmetic and copies ran while one was open for 35% -> 15% of each run, Pallas kernels for 0% -> 0%
where the time goes in v1:
time: 1080 us; the launch traced here: 1070 us
  local copies, waits for them, and re-layouts  358 us (33%)
  starting transfers between devices  317 us (29%)
  other arithmetic  203 us (19%)
  waiting for transfers between devices  165 us (15%)
  between operations  17.6 us (2%)
    ppermute x39, starting transfers between devices, extended_2(): lax.ppermute(lax.slice_in_dim(block, block.shape[dim] - width, None, axis...  160 us
    reduce_scatter x1, waiting for transfers between devices, local(): lax.psum_scatter(region_partial, ('gx', 'gy', 'gz'), scatter_dimension=1,...  141 us
    gather x20, local copies, waits for them, and re-layouts, fault_sum(): own_values = flattened[:, cell_index]  125 us
    scatter-add x10, other arithmetic, fault_sum(): faults = jnp.zeros((flattened.shape[1],), jnp.float32).at[cell_index.resh...  115 us
    all_to_all x10, starting transfers between devices, fault_exchange(): lax.all_to_all(jnp.stack(jnp.split(values, lax.axis_size(('gy', 'gz')), a...  100 us
    unnamed x378, local copies, waits for them, and re-layouts  90.8 us
    ppermute x39, starting transfers between devices, extended_2(): lax.ppermute(lax.slice_in_dim(block, 0, width, axis=dim), axis, backward)  51.1 us
    reshape x10, local copies, waits for them, and re-layouts, fault_sum(): flattened = lagrange.reshape(lagrange.shape[0], -1)  47.4 us
  transfers between devices with their start and end apart: 90, of which 21 were waited for; matrix products, arithmetic and copies ran while one was open for 15% of the time, Pallas kernels for 0%

profile of v1, /device:TPU:0, one launch (start us, length us, event | category | flops | bytes accessed | tf_op | source)
XLA Modules:
  0.0 1069.3 jit_solution(17115476830173005751)
XLA Ops:
  18.0 8.5 psum.7
  41.2 11.0 %gather_fusion.8 = f32[2048,3]{1,0:T(8,128)} fusion(f32[3,16384]{0,1:T(8,128)} %bitcast.1089, s32[2048]{0:T(1024)S(1)} %fusion.272), kind=kCustom, calls=%fused_computation.8 | custom fusion | bytes 57344 | tf_op jit(solution)/shard_map/gather | solution.py:73
  92.9 11.0 %gather_fusion.7 = f32[2048,6]{1,0:T(8,128)} fusion(f32[6,16384]{0,1:T(8,128)} %copy.813, s32[2048]{0:T(1024)S(1)} %fusion.272), kind=kCustom, calls=%fused_computation.7 | custom fusion | bytes 106496 | tf_op jit(solution)/shard_map/gather | solution.py:177
  155.3 12.0 %scatter_custom_fusion.1 = f32[16384]{0:T(1024)} fusion(s32[2048]{0:T(1024)} %bitcast.1299, f32[2048]{0:T(1024)S(1)} %bitcast.1298, f32[]{:T(128)} %constant.81.clone.1), kind=kCustom, calls=%fused_computation.872 | custom fusion | flops 2048 | bytes 66048 | tf_op jit(solution)/shard_map/scatter-add | solution.py:79
  201.0 11.0 %gather_fusion.9 = f32[2048,3]{1,0:T(8,128)} fusion(f32[3,16384]{0,1:T(8,128)} %bitcast.1082, s32[2048]{0:T(1024)S(1)} %fusion.272), kind=kCustom, calls=%fused_computation.9 | custom fusion | bytes 57344 | tf_op jit(solution)/shard_map/gather | solution.py:73
  249.2 11.4 %scatter_custom_fusion.2 = f32[16384]{0:T(1024)S(1)} fusion(s32[2048]{0:T(1024)} %bitcast.1300, f32[2048]{0:T(1024)S(1)} %bitcast.1311, f32[]{:T(128)} %constant.81.clone.1), kind=kCustom, calls=%fused_computation.870 | custom fusion | flops 2048 | bytes 66048 | tf_op jit(solution)/shard_map/scatter-add | solution.py:79
  266.6 10.9 %gather_fusion.10 = f32[2048,3]{1,0:T(8,128)} fusion(f32[3,16384]{0,1:T(8,128)} %bitcast.1083, s32[2048]{0:T(1024)S(1)} %fusion.272), kind=kCustom, calls=%fused_computation.10 | custom fusion | bytes 57344 | tf_op jit(solution)/shard_map/gather | solution.py:73
  301.8 11.5 %all-to-all-start.3 = ((f32[16,3,1,128]{3,2,1,0:T(1,128)}), f32[16,3,1,128]{3,2,1,0:T(1,128)}, u32[]{:S(2)}, u32[]{:S(2)}) async-start(f32[16,3,1,128]{3,2,1,0:T(1,128)} %constant_dynamic-update-slice_fusion.41), calls=%async_computation.3 | async-start | bytes 49152 | tf_op jit(solution)/shard_map/all_to_all | solution.py:64
  321.3 11.6 %scatter_custom_fusion.3 = f32[16384]{0:T(1024)S(1)} fusion(s32[2048]{0:T(1024)} %bitcast.1301, f32[2048]{0:T(1024)S(1)} %bitcast.1312, f32[]{:T(128)} %constant.81.clone.1), kind=kCustom, calls=%fused_computation.868 | custom fusion | flops 2048 | bytes 66048 | tf_op jit(solution)/shard_map/scatter-add | solution.py:79
  338.8 10.9 %gather_fusion.11 = f32[2048,3]{1,0:T(8,128)} fusion(f32[3,16384]{0,1:T(8,128)} %bitcast.1084, s32[2048]{0:T(1024)S(1)} %fusion.272), kind=kCustom, calls=%fused_computation.11 | custom fusion | bytes 57344 | tf_op jit(solution)/shard_map/gather | solution.py:73
  373.7 11.2 %all-to-all-start.4 = ((f32[16,3,1,128]{3,2,1,0:T(1,128)}), f32[16,3,1,128]{3,2,1,0:T(1,128)}, u32[]{:S(2)}, u32[]{:S(2)}) async-start(f32[16,3,1,128]{3,2,1,0:T(1,128)} %constant_dynamic-update-slice_fusion.57), calls=%async_computation.4 | async-start | bytes 49152 | tf_op jit(solution)/shard_map/all_to_all | solution.py:64
  393.0 11.4 %scatter_custom_fusion.4 = f32[16384]{0:T(1024)S(1)} fusion(s32[2048]{0:T(1024)} %bitcast.1302, f32[2048]{0:T(1024)S(1)} %bitcast.1313, f32[]{:T(128)} %constant.81.clone.1), kind=kCustom, calls=%fused_computation.866 | custom fusion | flops 2048 | bytes 66048 | tf_op jit(solution)/shard_map/scatter-add | solution.py:79
  410.3 10.9 %gather_fusion.12 = f32[2048,3]{1,0:T(8,128)} fusion(f32[3,16384]{0,1:T(8,128)} %bitcast.1085, s32[2048]{0:T(1024)S(1)} %fusion.272), kind=kCustom, calls=%fused_computation.12 | custom fusion | bytes 57344 | tf_op jit(solution)/shard_map/gather | solution.py:73
  445.2 11.2 %all-to-all-start.5 = ((f32[16,3,1,128]{3,2,1,0:T(1,128)}), f32[16,3,1,128]{3,2,1,0:T(1,128)}, u32[]{:S(2)}, u32[]{:S(2)}) async-start(f32[16,3,1,128]{3,2,1,0:T(1,128)} %constant_dynamic-update-slice_fusion.73), calls=%async_computation.5 | async-start | bytes 49152 | tf_op jit(solution)/shard_map/all_to_all | solution.py:64
  464.5 11.4 %scatter_custom_fusion.5 = f32[16384]{0:T(1024)S(1)} fusion(s32[2048]{0:T(1024)} %bitcast.1303, f32[2048]{0:T(1024)S(1)} %bitcast.1310, f32[]{:T(128)} %constant.81.clone.1), kind=kCustom, calls=%fused_computation.864 | custom fusion | flops 2048 | bytes 66048 | tf_op jit(solution)/shard_map/scatter-add | solution.py:79
  495.0 10.9 %gather_fusion.15 = f32[2048,3]{1,0:T(8,128)} fusion(f32[3,16384]{0,1:T(8,128)} %bitcast.1080, s32[2048]{0:T(1024)S(1)} %fusion.272), kind=kCustom, calls=%fused_computation.15 | custom fusion | bytes 57344 | tf_op jit(solution)/shard_map/gather | solution.py:73
  518.4 12.1 %all-to-all-start.6 = ((f32[16,3,1,128]{3,2,1,0:T(1,128)}), f32[16,3,1,128]{3,2,1,0:T(1,128)}, u32[]{:S(2)}, u32[]{:S(2)}) async-start(f32[16,3,1,128]{3,2,1,0:T(1,128)} %constant_dynamic-update-slice_fusion.89), calls=%async_computation.6 | async-start | bytes 49152 | tf_op jit(solution)/shard_map/all_to_all | solution.py:64
  574.0 11.4 %scatter_custom_fusion.7 = f32[16384]{0:T(1024)S(1)} fusion(s32[2048]{0:T(1024)} %bitcast.1304, f32[2048]{0:T(1024)S(1)} %bitcast.1297, f32[]{:T(128)} %constant.81.clone.1), kind=kCustom, calls=%fused_computation.862 | custom fusion | flops 2048 | bytes 66048 | tf_op jit(solution)/shard_map/scatter-add | solution.py:79
  591.3 10.9 %gather_fusion.16 = f32[2048,3]{1,0:T(8,128)} fusion(f32[3,16384]{0,1:T(8,128)} %bitcast.1086, s32[2048]{0:T(1024)S(1)} %fusion.272), kind=kCustom, calls=%fused_computation.16 | custom fusion | bytes 57344 | tf_op jit(solution)/shard_map/gather | solution.py:73
  625.6 11.1 %all-to-all-start.7 = ((f32[16,3,1,128]{3,2,1,0:T(1,128)}), f32[16,3,1,128]{3,2,1,0:T(1,128)S(1)}, u32[]{:S(2)}, u32[]{:S(2)}) async-start(f32[16,3,1,128]{3,2,1,0:T(1,128)} %constant_dynamic-update-slice_fusion.105), calls=%async_computation.7 | async-start | bytes 49152 | tf_op jit(solution)/shard_map/all_to_all | solution.py:64
  644.0 11.6 %scatter_custom_fusion.8 = f32[16384]{0:T(1024)S(1)} fusion(s32[2048]{0:T(1024)} %bitcast.1305, f32[2048]{0:T(1024)S(1)} %bitcast.1314, f32[]{:T(128)} %constant.81.clone.1), kind=kCustom, calls=%fused_computation.860 | custom fusion | flops 2048 | bytes 66048 | tf_op jit(solution)/shard_map/scatter-add | solution.py:79
  661.5 10.9 %gather_fusion.17 = f32[2048,3]{1,0:T(8,128)} fusion(f32[3,16384]{0,1:T(8,128)} %bitcast.1087, s32[2048]{0:T(1024)S(1)} %fusion.272), kind=kCustom, calls=%fused_computation.17 | custom fusion | bytes 57344 | tf_op jit(solution)/shard_map/gather | solution.py:73
  695.8 11.2 %all-to-all-start.8 = ((f32[16,3,1,128]{3,2,1,0:T(1,128)}), f32[16,3,1,128]{3,2,1,0:T(1,128)S(1)}, u32[]{:S(2)}, u32[]{:S(2)}) async-start(f32[16,3,1,128]{3,2,1,0:T(1,128)} %constant_dynamic-update-slice_fusion.121), calls=%async_computation.8 | async-start | bytes 49152 | tf_op jit(solution)/shard_map/all_to_all | solution.py:64
  714.4 11.4 %scatter_custom_fusion.9 = f32[16384]{0:T(1024)S(1)} fusion(s32[2048]{0:T(1024)} %bitcast.1306, f32[2048]{0:T(1024)S(1)} %bitcast.1315, f32[]{:T(128)} %constant.81.clone.1), kind=kCustom, calls=%fused_computation.858 | custom fusion | flops 2048 | bytes 66048 | tf_op jit(solution)/shard_map/scatter-add | solution.py:79
  731.7 10.9 %gather_fusion.18 = f32[2048,3]{1,0:T(8,128)} fusion(f32[3,16384]{0,1:T(8,128)} %bitcast.1088, s32[2048]{0:T(1024)S(1)} %fusion.272), kind=kCustom, calls=%fused_computation.18 | custom fusion | bytes 57344 | tf_op jit(solution)/shard_map/gather | solution.py:73
  765.9 11.2 %all-to-all-start.9 = ((f32[16,3,1,128]{3,2,1,0:T(1,128)}), f32[16,3,1,128]{3,2,1,0:T(1,128)S(1)}, u32[]{:S(2)}, u32[]{:S(2)}) async-start(f32[16,3,1,128]{3,2,1,0:T(1,128)} %constant_dynamic-update-slice_fusion.137), calls=%async_computation.9 | async-start | bytes 49152 | tf_op jit(solution)/shard_map/all_to_all | solution.py:64
  784.5 11.4 %scatter_custom_fusion.10 = f32[16384]{0:T(1024)S(1)} fusion(s32[2048]{0:T(1024)} %bitcast.1307, f32[2048]{0:T(1024)S(1)} %bitcast.1316, f32[]{:T(128)} %constant.81.clone.1), kind=kCustom, calls=%fused_computation.856 | custom fusion | flops 2048 | bytes 66048 | tf_op jit(solution)/shard_map/scatter-add | solution.py:79
  801.8 10.9 %gather_fusion.19 = f32[2048,3]{1,0:T(8,128)} fusion(f32[3,16384]{0,1:T(8,128)} %bitcast.1081, s32[2048]{0:T(1024)S(1)} %fusion.272), kind=kCustom, calls=%fused_computation.19 | custom fusion | bytes 57344 | tf_op jit(solution)/shard_map/gather | solution.py:73
  835.9 11.3 %all-to-all-start.10 = ((f32[16,3,1,128]{3,2,1,0:T(1,128)}), f32[16,3,1,128]{3,2,1,0:T(1,128)}, u32[]{:S(2)}, u32[]{:S(2)}) async-start(f32[16,3,1,128]{3,2,1,0:T(1,128)} %constant_dynamic-update-slice_fusion.153), calls=%async_computation.10 | async-start | bytes 49152 | tf_op jit(solution)/shard_map/all_to_all | solution.py:64
  854.6 11.4 %scatter_custom_fusion.11 = f32[16384]{0:T(1024)S(1)} fusion(s32[2048]{0:T(1024)} %bitcast.1308, f32[2048]{0:T(1024)S(1)} %bitcast.1309, f32[]{:T(128)} %constant.81.clone.1), kind=kCustom, calls=%fused_computation.854 | custom fusion | flops 2048 | bytes 66048 | tf_op jit(solution)/shard_map/scatter-add | solution.py:79
  889.7 9.6 add_reduce_fusion
  919.9 141.0 %reduce-scatter.2.cloned.1.call-done = f32[2,32]{0,1:T(8,128)} async-done(((f32[2,1024]{0,1:T(8,128)}), f32[2,32]{0,1:T(8,128)}) %reduce-scatter.2.cloned.1.call-update) | async-done | bytes 272 | tf_op jit(solution)/shard_map/reduce_scatter | solution.py:287
  (821 shorter events, 566.2 us)
Async XLA Ops:
  63.0 78.0 %all-to-all-start.1 = ((f32[16,3,1,128]{3,2,1,0:T(1,128)}), f32[16,3,1,128]{3,2,1,0:T(1,128)}, u32[]{:S(2)}, u32[]{:S(2)}) async-start(f32[16,3,1,128]{3,2,1,0:T(1,128)} %constant_dynamic-update-slice_fusion.9), calls=%async_computation.1 | async-start | bytes 49152 | tf_op jit(solution)/shard_map/all_to_all | solution.py:64
  74.6 61.1 %collective-permute-start = (f32[10,1,8,128]{3,2,1,0:T(8,128)}, f32[10,1,8,128]{3,2,1,0:T(8,128)S(1)}, u32[]{:S(2)}, u32[]{:S(2)}) collective-permute-start(f32[10,1,8,128]{3,2,1,0:T(8,128)} %get-tuple-element.156), channel_id=1, source_target_pairs={{0,16},{1,17},{2,18},{3,19},{4,20},{5,21},{6,22},{7,23},{8,24},{9,... | collective-permute-start | bytes 122888 | tf_op jit(solution)/shard_map/ppermute | solution.py:18
  75.8 59.8 %collective-permute-start.1 = (f32[10,1,8,128]{3,2,1,0:T(8,128)}, f32[10,1,8,128]{3,2,1,0:T(8,128)S(1)}, u32[]{:S(2)}, u32[]{:S(2)}) collective-permute-start(f32[10,1,8,128]{3,2,1,0:T(8,128)} %get-tuple-element.157), channel_id=1, source_target_pairs={{16,0},{17,1},{18,2},{19,3},{20,4},{21,5},{22,6},{23,7},{24,8},{25... | collective-permute-start | bytes 122888 | tf_op jit(solution)/shard_map/ppermute | solution.py:21
  79.8 49.5 %collective-permute-start.6 = (f32[3,18,1,128]{3,2,1,0:T(1,128)}, f32[3,18,1,128]{3,2,1,0:T(1,128)S(1)}, u32[]{:S(2)}, u32[]{:S(2)}) collective-permute-start(f32[3,18,1,128]{3,2,1,0:T(1,128)} %get-tuple-element.229), channel_id=1, source_target_pairs={{4,0},{8,4},{12,8},{5,1},{9,5},{13,9},{6,2},{10,6},{14,10},{7,3},{... | collective-permute-start | bytes 82952 | tf_op jit(solution)/shard_map/ppermute | solution.py:21
  81.1 48.2 %collective-permute-start.7 = (f32[3,18,1,128]{3,2,1,0:T(1,128)}, f32[3,18,1,128]{3,2,1,0:T(1,128)S(1)}, u32[]{:S(2)}, u32[]{:S(2)}) collective-permute-start(f32[3,18,1,128]{3,2,1,0:T(1,128)} %get-tuple-element.228), channel_id=1, source_target_pairs={{0,4},{4,8},{8,12},{1,5},{5,9},{9,13},{2,6},{6,10},{10,14},{3,7},{... | collective-permute-start | bytes 82952 | tf_op jit(solution)/shard_map/ppermute | solution.py:18
  130.4 59.4 %collective-permute-start.10 = (f32[3,18,10,1]{3,2,1,0:T(8,128)}, f32[3,18,10,1]{3,2,1,0:T(8,128)}, u32[]{:S(2)}, u32[]{:S(2)}) collective-permute-start(f32[3,18,10,1]{3,2,1,0:T(8,128)} %get-tuple-element.181), channel_id=1, source_target_pairs={{1,0},{2,1},{3,2},{5,4},{6,5},{7,6},{9,8},{10,9},{11,10},{13,12},{... | collective-permute-start | bytes 6488 | tf_op jit(solution)/shard_map/ppermute | solution.py:21
  131.8 58.0 %collective-permute-start.11 = (f32[3,18,10,1]{3,2,1,0:T(8,128)}, f32[3,18,10,1]{3,2,1,0:T(8,128)}, u32[]{:S(2)}, u32[]{:S(2)}) collective-permute-start(f32[3,18,10,1]{3,2,1,0:T(8,128)} %get-tuple-element.180), channel_id=1, source_target_pairs={{0,1},{1,2},{2,3},{4,5},{5,6},{6,7},{8,9},{9,10},{10,11},{12,13},{... | collective-permute-start | bytes 6488 | tf_op jit(solution)/shard_map/ppermute | solution.py:18
  135.8 31.5 %collective-permute-start.4 = (f32[10,18,1,128]{3,2,1,0:T(1,128)S(1)}, f32[10,18,1,128]{3,2,1,0:T(1,128)S(1)}, u32[]{:S(2)}, u32[]{:S(2)}) collective-permute-start(f32[10,18,1,128]{3,2,1,0:T(1,128)S(1)} %get-tuple-element.154), channel_id=1, source_target_pairs={{0,4},{4,8},{8,12},{1,5},{5,9},{9,13},{2,6},{6,10},{10,14},{3,7},{... | collective-permute-start | bytes 276488 | tf_op jit(solution)/shard_map/ppermute | solution.py:18
  139.6 27.8 %collective-permute-start.5 = (f32[10,18,1,128]{3,2,1,0:T(1,128)S(1)}, f32[10,18,1,128]{3,2,1,0:T(1,128)S(1)}, u32[]{:S(2)}, u32[]{:S(2)}) collective-permute-start(f32[10,18,1,128]{3,2,1,0:T(1,128)S(1)} %get-tuple-element.155), channel_id=1, source_target_pairs={{4,0},{8,4},{12,8},{5,1},{9,5},{13,9},{6,2},{10,6},{14,10},{7,3},{... | collective-permute-start | bytes 276488 | tf_op jit(solution)/shard_map/ppermute | solution.py:21
  222.8 26.4 %all-to-all-start.2 = ((f32[16,3,1,128]{3,2,1,0:T(1,128)}), f32[16,3,1,128]{3,2,1,0:T(1,128)S(1)}, u32[]{:S(2)}, u32[]{:S(2)}) async-start(f32[16,3,1,128]{3,2,1,0:T(1,128)} %constant_dynamic-update-slice_fusion.25), calls=%async_computation.2 | async-start | bytes 49152 | tf_op jit(solution)/shard_map/all_to_all | solution.py:64
  295.0 18.2 %collective-permute-start.20 = (f32[3,18,1,128]{3,2,1,0:T(1,128)}, f32[3,18,1,128]{3,2,1,0:T(1,128)S(1)}, u32[]{:S(2)}, u32[]{:S(2)}) collective-permute-start(f32[3,18,1,128]{3,2,1,0:T(1,128)} %get-tuple-element.225), channel_id=1, source_target_pairs={{4,0},{8,4},{12,8},{5,1},{9,5},{13,9},{6,2},{10,6},{14,10},{7,3},{... | collective-permute-start | bytes 82952 | tf_op jit(solution)/shard_map/ppermute | solution.py:21
  296.3 16.9 %collective-permute-start.21 = (f32[3,18,1,128]{3,2,1,0:T(1,128)}, f32[3,18,1,128]{3,2,1,0:T(1,128)S(1)}, u32[]{:S(2)}, u32[]{:S(2)}) collective-permute-start(f32[3,18,1,128]{3,2,1,0:T(1,128)} %get-tuple-element.224), channel_id=1, source_target_pairs={{0,4},{4,8},{8,12},{1,5},{5,9},{9,13},{2,6},{6,10},{10,14},{3,7},{... | collective-permute-start | bytes 82952 | tf_op jit(solution)/shard_map/ppermute | solution.py:18
  301.8 18.8 %all-to-all-start.3 = ((f32[16,3,1,128]{3,2,1,0:T(1,128)}), f32[16,3,1,128]{3,2,1,0:T(1,128)}, u32[]{:S(2)}, u32[]{:S(2)}) async-start(f32[16,3,1,128]{3,2,1,0:T(1,128)} %constant_dynamic-update-slice_fusion.41), calls=%async_computation.3 | async-start | bytes 49152 | tf_op jit(solution)/shard_map/all_to_all | solution.py:64
  367.3 17.7 %collective-permute-start.26 = (f32[3,18,1,128]{3,2,1,0:T(1,128)}, f32[3,18,1,128]{3,2,1,0:T(1,128)S(1)}, u32[]{:S(2)}, u32[]{:S(2)}) collective-permute-start(f32[3,18,1,128]{3,2,1,0:T(1,128)} %get-tuple-element.223), channel_id=1, source_target_pairs={{4,0},{8,4},{12,8},{5,1},{9,5},{13,9},{6,2},{10,6},{14,10},{7,3},{... | collective-permute-start | bytes 82952 | tf_op jit(solution)/shard_map/ppermute | solution.py:21
  373.7 18.5 %all-to-all-start.4 = ((f32[16,3,1,128]{3,2,1,0:T(1,128)}), f32[16,3,1,128]{3,2,1,0:T(1,128)}, u32[]{:S(2)}, u32[]{:S(2)}) async-start(f32[16,3,1,128]{3,2,1,0:T(1,128)} %constant_dynamic-update-slice_fusion.57), calls=%async_computation.4 | async-start | bytes 49152 | tf_op jit(solution)/shard_map/all_to_all | solution.py:64
  438.8 17.7 %collective-permute-start.32 = (f32[3,18,1,128]{3,2,1,0:T(1,128)}, f32[3,18,1,128]{3,2,1,0:T(1,128)S(1)}, u32[]{:S(2)}, u32[]{:S(2)}) collective-permute-start(f32[3,18,1,128]{3,2,1,0:T(1,128)} %get-tuple-element.221), channel_id=1, source_target_pairs={{4,0},{8,4},{12,8},{5,1},{9,5},{13,9},{6,2},{10,6},{14,10},{7,3},{... | collective-permute-start | bytes 82952 | tf_op jit(solution)/shard_map/ppermute | solution.py:21
  445.2 18.5 %all-to-all-start.5 = ((f32[16,3,1,128]{3,2,1,0:T(1,128)}), f32[16,3,1,128]{3,2,1,0:T(1,128)}, u32[]{:S(2)}, u32[]{:S(2)}) async-start(f32[16,3,1,128]{3,2,1,0:T(1,128)} %constant_dynamic-update-slice_fusion.73), calls=%async_computation.5 | async-start | bytes 49152 | tf_op jit(solution)/shard_map/all_to_all | solution.py:64
  489.1 58.1 %collective-permute-start.66 = (f32[3,1,8,128]{3,2,1,0:T(8,128)}, f32[3,1,8,128]{3,2,1,0:T(8,128)S(1)}, u32[]{:S(2)}, u32[]{:S(2)}) collective-permute-start(f32[3,1,8,128]{3,2,1,0:T(8,128)} %get-tuple-element.231), channel_id=1, source_target_pairs={{16,0},{17,1},{18,2},{19,3},{20,4},{21,5},{22,6},{23,7},{24,8},{25... | collective-permute-start | bytes 36872 | tf_op jit(solution)/shard_map/ppermute | solution.py:21
  490.4 56.8 %collective-permute-start.67 = (f32[3,1,8,128]{3,2,1,0:T(8,128)}, f32[3,1,8,128]{3,2,1,0:T(8,128)S(1)}, u32[]{:S(2)}, u32[]{:S(2)}) collective-permute-start(f32[3,1,8,128]{3,2,1,0:T(8,128)} %get-tuple-element.230), channel_id=1, source_target_pairs={{0,16},{1,17},{2,18},{3,19},{4,20},{5,21},{6,22},{7,23},{8,24},{9,... | collective-permute-start | bytes 36872 | tf_op jit(solution)/shard_map/ppermute | solution.py:18
  518.4 54.7 %all-to-all-start.6 = ((f32[16,3,1,128]{3,2,1,0:T(1,128)}), f32[16,3,1,128]{3,2,1,0:T(1,128)}, u32[]{:S(2)}, u32[]{:S(2)}) async-start(f32[16,3,1,128]{3,2,1,0:T(1,128)} %constant_dynamic-update-slice_fusion.89), calls=%async_computation.6 | async-start | bytes 49152 | tf_op jit(solution)/shard_map/all_to_all | solution.py:64
  530.5 22.6 %collective-permute-start.36 = (f32[3,1,8,128]{3,2,1,0:T(8,128)S(1)}, f32[3,1,8,128]{3,2,1,0:T(8,128)S(1)}, u32[]{:S(2)}, u32[]{:S(2)}) collective-permute-start(f32[3,1,8,128]{3,2,1,0:T(8,128)S(1)} %get-tuple-element.249), channel_id=1, source_target_pairs={{16,0},{17,1},{18,2},{19,3},{20,4},{21,5},{22,6},{23,7},{24,8},{25... | collective-permute-start | bytes 36872 | tf_op jit(solution)/shard_map/ppermute | solution.py:21
  531.8 21.3 %collective-permute-start.37 = (f32[3,1,8,128]{3,2,1,0:T(8,128)S(1)}, f32[3,1,8,128]{3,2,1,0:T(8,128)S(1)}, u32[]{:S(2)}, u32[]{:S(2)}) collective-permute-start(f32[3,1,8,128]{3,2,1,0:T(8,128)S(1)} %get-tuple-element.248), channel_id=1, source_target_pairs={{0,16},{1,17},{2,18},{3,19},{4,20},{5,21},{6,22},{7,23},{8,24},{9,... | collective-permute-start | bytes 36872 | tf_op jit(solution)/shard_map/ppermute | solution.py:18
  619.2 17.6 %collective-permute-start.44 = (f32[3,18,1,128]{3,2,1,0:T(1,128)S(1)}, f32[3,18,1,128]{3,2,1,0:T(1,128)S(1)}, u32[]{:S(2)}, u32[]{:S(2)}) collective-permute-start(f32[3,18,1,128]{3,2,1,0:T(1,128)S(1)} %get-tuple-element.217), channel_id=1, source_target_pairs={{4,0},{8,4},{12,8},{5,1},{9,5},{13,9},{6,2},{10,6},{14,10},{7,3},{... | collective-permute-start | bytes 82952 | tf_op jit(solution)/shard_map/ppermute | solution.py:21
  625.6 18.4 %all-to-all-start.7 = ((f32[16,3,1,128]{3,2,1,0:T(1,128)}), f32[16,3,1,128]{3,2,1,0:T(1,128)S(1)}, u32[]{:S(2)}, u32[]{:S(2)}) async-start(f32[16,3,1,128]{3,2,1,0:T(1,128)} %constant_dynamic-update-slice_fusion.105), calls=%async_computation.7 | async-start | bytes 49152 | tf_op jit(solution)/shard_map/all_to_all | solution.py:64
  689.4 17.7 %collective-permute-start.50 = (f32[3,18,1,128]{3,2,1,0:T(1,128)S(1)}, f32[3,18,1,128]{3,2,1,0:T(1,128)S(1)}, u32[]{:S(2)}, u32[]{:S(2)}) collective-permute-start(f32[3,18,1,128]{3,2,1,0:T(1,128)S(1)} %get-tuple-element.215), channel_id=1, source_target_pairs={{4,0},{8,4},{12,8},{5,1},{9,5},{13,9},{6,2},{10,6},{14,10},{7,3},{... | collective-permute-start | bytes 82952 | tf_op jit(solution)/shard_map/ppermute | solution.py:21
  695.8 18.5 %all-to-all-start.8 = ((f32[16,3,1,128]{3,2,1,0:T(1,128)}), f32[16,3,1,128]{3,2,1,0:T(1,128)S(1)}, u32[]{:S(2)}, u32[]{:S(2)}) async-start(f32[16,3,1,128]{3,2,1,0:T(1,128)} %constant_dynamic-update-slice_fusion.121), calls=%async_computation.8 | async-start | bytes 49152 | tf_op jit(solution)/shard_map/all_to_all | solution.py:64
  759.5 17.7 %collective-permute-start.56 = (f32[3,18,1,128]{3,2,1,0:T(1,128)S(1)}, f32[3,18,1,128]{3,2,1,0:T(1,128)S(1)}, u32[]{:S(2)}, u32[]{:S(2)}) collective-permute-start(f32[3,18,1,128]{3,2,1,0:T(1,128)S(1)} %get-tuple-element.213), channel_id=1, source_target_pairs={{4,0},{8,4},{12,8},{5,1},{9,5},{13,9},{6,2},{10,6},{14,10},{7,3},{... | collective-permute-start | bytes 82952 | tf_op jit(solution)/shard_map/ppermute | solution.py:21
  765.9 18.5 %all-to-all-start.9 = ((f32[16,3,1,128]{3,2,1,0:T(1,128)}), f32[16,3,1,128]{3,2,1,0:T(1,128)S(1)}, u32[]{:S(2)}, u32[]{:S(2)}) async-start(f32[16,3,1,128]{3,2,1,0:T(1,128)} %constant_dynamic-update-slice_fusion.137), calls=%async_computation.9 | async-start | bytes 49152 | tf_op jit(solution)/shard_map/all_to_all | solution.py:64
  829.5 17.7 %collective-permute-start.62 = (f32[3,18,1,128]{3,2,1,0:T(1,128)S(1)}, f32[3,18,1,128]{3,2,1,0:T(1,128)S(1)}, u32[]{:S(2)}, u32[]{:S(2)}) collective-permute-start(f32[3,18,1,128]{3,2,1,0:T(1,128)S(1)} %get-tuple-element.211), channel_id=1, source_target_pairs={{4,0},{8,4},{12,8},{5,1},{9,5},{13,9},{6,2},{10,6},{14,10},{7,3},{... | collective-permute-start | bytes 82952 | tf_op jit(solution)/shard_map/ppermute | solution.py:21
  835.9 17.9 %all-to-all-start.10 = ((f32[16,3,1,128]{3,2,1,0:T(1,128)}), f32[16,3,1,128]{3,2,1,0:T(1,128)}, u32[]{:S(2)}, u32[]{:S(2)}) async-start(f32[16,3,1,128]{3,2,1,0:T(1,128)} %constant_dynamic-update-slice_fusion.153), calls=%async_computation.10 | async-start | bytes 49152 | tf_op jit(solution)/shard_map/all_to_all | solution.py:64
  847.2 213.6 %reduce-scatter.2.cloned.1.call-start = ((), (), s32[]{:S(2)}) async-start(), calls=%async_computation.12 | async-start | bytes 540672 | tf_op jit(solution)/shard_map/reduce_scatter | solution.py:287
  867.3 16.5 %collective-permute-start.72 = (f32[3,1,8,128]{3,2,1,0:T(8,128)S(1)}, f32[3,1,8,128]{3,2,1,0:T(8,128)S(1)}, u32[]{:S(2)}, u32[]{:S(2)}) collective-permute-start(f32[3,1,8,128]{3,2,1,0:T(8,128)S(1)} %get-tuple-element.233), channel_id=1, source_target_pairs={{16,0},{17,1},{18,2},{19,3},{20,4},{21,5},{22,6},{23,7},{24,8},{25... | collective-permute-start | bytes 36872 | tf_op jit(solution)/shard_map/ppermute | solution.py:21
  (171 other events, 2125.7 us)
Sparse Core Ops, SparseCore 0:
  919.2 141.5 reduce-scatter.1
